TPU v7x, 32 devices: a whole 2x2x4 slice. The times are simulated.
32 devices in a mesh: dp: 2 (over x), ctx: 4 (over z), mp: 4 (over y, core).
Axes of the slice: x: 2, y: 2, z: 4, core: 2. Of those that a mesh axis runs over, the one named last changes fastest.
Arguments:
- inputs: bfloat16 [1, 1024, 2048], P(None, ('dp', 'ctx'), 'mp'), may hold values from -6 to 6
- doc_start: int32 [1, 1024], P(None, ('dp', 'ctx')), may hold values 0 or 1
- gate_weight: bfloat16 [256, 8, 512], P(None, 'mp'), may hold values from -0.375 to 0.375
- gate_bias: float32 [8, 512], P('mp'), may hold values from -4 to 4
- decay_rate: float32 [2048], P('mp'), may hold values from 1.953125e-05 to 0.08, as said below
- cotangent: bfloat16 [1, 1024, 2048], P(None, ('dp', 'ctx'), 'mp'), may hold values from -0.59765625 to 0.59765625
Outputs:
- outputs: bfloat16 [1, 1024, 2048], P(None, ('dp', 'ctx'), 'mp')
- grad_inputs: bfloat16 [1, 1024, 2048], P(None, ('dp', 'ctx'), 'mp')
- grad_gate_weight: float32 [256, 8, 512], P(('dp', 'ctx'), 'mp')
Inputs may be any that keep to these rules, and one draw needn't show every extreme that they name: `decay_rate`: each channel's rate is either slow, between 0.02 / 1024 and 0.2 / 1024, or fast, between 0.02 and 0.08, in any mix.
All inputs are finite; a program needn't handle non-finite values. No bound on the sum of `doc_start` on one device may be relied on, other than what follows from the above.
Results may differ from a plain program's by a relative error of at most 0.0028.
Values sent between devices are 32-bit elements; how exact they have to be, the bound alone decides.
A program may use at most 64 MiB of HBM per device.

v0:
```python
import functools

import jax
import jax.numpy as jnp
from jax import lax
from jax.experimental import pallas as pl
from jax.experimental.pallas import tpu as pltpu
from jax.sharding import PartitionSpec as P

MESH = pl.DeviceIdType.MESH
SUB = 8


def kernel(
    dps, ctxs, x_ref, doc_ref, w_ref, bias_ref, rate_ref, g_ref, out_ref, gx_ref, gw_ref,
    xf, xb, xt, gf, pre, carry_s, s_s, p_s, la_s, q_s, c1a_s, c1b_s, c2_s, c3_s, outp, dpre,
    gxp, sums, sums_in, gwp, recv1, sbuf, recv2,
    sum_send, sum_recv, one_send, one_recv, two_send, two_recv,
):
    rows, width = x_ref.shape
    heads, hd, hm = w_ref.shape
    count = dps * ctxs
    steps = rows // SUB
    my_dp, my_ctx = lax.axis_index("dp"), lax.axis_index("ctx")
    me = my_dp * ctxs + my_ctx
    f32, bf16 = jnp.float32, jnp.bfloat16

    barrier = pltpu.get_barrier_semaphore()
    for d in range(1, count):
        to = lax.rem(me + d, count)
        pl.semaphore_signal(
            barrier, inc=1, device_id={"dp": to // ctxs, "ctx": lax.rem(to, ctxs)},
            device_id_type=MESH,
        )

    row = lax.broadcasted_iota(jnp.int32, (rows, rows), 0)
    col = lax.broadcasted_iota(jnp.int32, (rows, rows), 1)
    here = (row % SUB) * steps + row // SUB == col
    back_here = (col % SUB) * steps + col // SUB == row
    perm = jnp.where(here, 1.0, 0.0).astype(bf16)
    unperm = jnp.where(back_here, 1.0, 0.0).astype(bf16)
    keep_col = 1.0 - jnp.sum(
        jnp.where(here, doc_ref[...].astype(f32), 0.0), axis=1, keepdims=True
    )
    xf[...] = jnp.dot(perm, x_ref[...], preferred_element_type=f32)
    xb[...] = xf[...].astype(bf16)
    gf[...] = jnp.dot(perm, g_ref[...], preferred_element_type=f32)
    chunk = lax.broadcasted_iota(jnp.int32, (SUB, hd), 0)

    ends = []
    for h in range(heads):
        ch = slice(h * hd, (h + 1) * hd)
        pre[...] = (
            jnp.dot(xb[:, ch], w_ref[h], preferred_element_type=f32) + bias_ref[h : h + 1, :]
        )
        rate8 = -8.0 * rate_ref[:, ch]
        state = prod = None
        for i in range(steps):
            rs = slice(i * SUB, (i + 1) * SUB)
            x = xf[rs, ch]
            keep = jnp.broadcast_to(keep_col[rs], (SUB, hd))
            kept = keep > 0.5
            rgate = 0.5 * jnp.tanh(0.5 * pre[rs, :hd]) + 0.5
            igate = 0.5 * jnp.tanh(0.5 * pre[rs, hd:]) + 0.5
            decay = jnp.exp(rate8 * rgate)
            square = decay * decay
            inside = 1.0 - square + 0.01
            inverse = lax.rsqrt(inside)
            carry = decay * keep
            scale = jnp.where(kept, inside * inverse, 1.0)
            c3 = scale * igate
            gated = igate * x
            drive = scale * gated
            c1 = rate8 * rgate * (1.0 - rgate)
            carry_s[rs, ch] = carry
            c1a_s[rs, ch] = carry * c1
            c1b_s[rs, ch] = gated * jnp.where(kept, -square * inverse, 0.0) * c1
            c2_s[rs, ch] = drive * (1.0 - igate)
            c3_s[rs, ch] = c3
            if i == 0:
                state, prod = drive, carry
            else:
                state, prod = carry * state + drive, carry * prod
            s_s[rs, ch] = state
            p_s[rs, ch] = prod
        adj = gf[(steps - 1) * SUB :, ch]
        tail = jnp.ones((SUB, hd), f32)
        la_s[(steps - 1) * SUB :, ch] = adj
        q_s[(steps - 1) * SUB :, ch] = tail
        for i in range(steps - 2, -1, -1):
            rs = slice(i * SUB, (i + 1) * SUB)
            after = carry_s[(i + 1) * SUB : (i + 2) * SUB, ch]
            adj = gf[rs, ch] + after * adj
            tail = after * tail
            la_s[rs, ch] = adj
            q_s[rs, ch] = tail
        first = carry_s[:SUB, ch]
        fs, fp = state, prod
        bu, bp = first * adj, prod
        s = 1
        while s < SUB:
            ok = chunk >= s
            rolled_p, rolled_s = pltpu.roll(fp, s, 0), pltpu.roll(fs, s, 0)
            fs = jnp.where(ok, fp * rolled_s + fs, fs)
            fp = jnp.where(ok, fp * rolled_p, fp)
            ok = chunk < SUB - s
            rolled_p, rolled_s = pltpu.roll(bp, SUB - s, 0), pltpu.roll(bu, SUB - s, 0)
            bu = jnp.where(ok, bp * rolled_s + bu, bu)
            bp = jnp.where(ok, bp * rolled_p, bp)
            s *= 2
        for l in range(hd // 128):
            lanes = slice(l * 128, (l + 1) * 128)
            at = h * (hd // 128) + l
            half = width // 128
            sums[0, at : at + 1] = fp[SUB - 1 :, lanes]
            sums[1, at : at + 1] = fp[SUB - 1 :, lanes]
            sums[0, half + at : half + at + 1] = bu[:1, lanes]
            sums[1, half + at : half + at + 1] = fs[SUB - 1 :, lanes]
        ends.append((
            jnp.where(chunk >= 1, pltpu.roll(fp, 1, 0), 1.0),
            jnp.where(chunk >= 1, pltpu.roll(fs, 1, 0), 0.0),
            jnp.where(chunk < SUB - 1, pltpu.roll(bp, SUB - 1, 0), 1.0),
            jnp.where(chunk < SUB - 1, pltpu.roll(bu, SUB - 1, 0), 0.0),
        ))

    pl.semaphore_wait(barrier, count - 1)
    sends = []
    summaries = []
    for d in range(1, count):
        to = lax.rem(me + d, count)
        copy = pltpu.make_async_remote_copy(
            src_ref=sums.at[(to - me + count) // count],
            dst_ref=sums_in.at[d - 1],
            send_sem=sum_send.at[d - 1],
            recv_sem=sum_recv.at[d - 1],
            device_id={"dp": to // ctxs, "ctx": lax.rem(to, ctxs)},
            device_id_type=MESH,
        )
        copy.start()
        sends.append(copy)
        summaries.append(copy)

    for h in range(heads):
        ch = slice(h * hd, (h + 1) * hd)
        xt[ch, :] = jnp.transpose(xf[:, ch]).astype(bf16)

    for copy in summaries:
        copy.wait_recv()
    half = width // 128
    state_in = jnp.zeros((half, 128), f32)
    adj_in = jnp.zeros((half, 128), f32)
    for d in range(count - 1, 0, -1):
        longer = sums_in[d - 1, :half] * state_in + sums_in[d - 1, half:]
        state_in = jnp.where(d <= me, longer, state_in)
        after = count - d - 1
        longer = sums_in[after, :half] * adj_in + sums_in[after, half:]
        adj_in = jnp.where(me + d < count, longer, adj_in)

    def lanes_of(value, h):
        per = hd // 128
        return jnp.concatenate([value[h * per + l : h * per + l + 1] for l in range(per)], axis=1)

    block = ctxs * (hd // count)
    stage_one = {}
    for h in range(heads):
        ch = slice(h * hd, (h + 1) * hd)
        ex_p, ex_s, ex_q, ex_u = ends[h]
        start = ex_s + ex_p * lanes_of(state_in, h)
        prev = start
        enter = ex_u + ex_q * lanes_of(adj_in, h)
        for i in range(0, steps, 2):
            got = []
            for j in (i, i + 1):
                rs = slice(j * SUB, (j + 1) * SUB)
                state = s_s[rs, ch] + p_s[rs, ch] * start
                adj = la_s[rs, ch] + q_s[rs, ch] * enter
                dgate = adj * (c1a_s[rs, ch] * prev + c1b_s[rs, ch])
                got.append((state, dgate, adj * c2_s[rs, ch], adj * c3_s[rs, ch]))
                prev = state
            both = slice(i * SUB, (i + 2) * SUB)
            outp[both, ch] = jnp.concatenate([got[0][0], got[1][0]]).astype(bf16)
            dpre[both, h * hm : h * hm + hd] = jnp.concatenate([got[0][1], got[1][1]]).astype(bf16)
            dpre[both, h * hm + hd : (h + 1) * hm] = jnp.concatenate(
                [got[0][2], got[1][2]]
            ).astype(bf16)
            gxp[both, ch] = jnp.concatenate([got[0][3], got[1][3]])
        for d in list(range(1, dps)) + [0]:
            to_dp = lax.rem(my_dp + d, dps)
            left = xt[pl.ds(pl.multiple_of(h * hd + to_dp * block, block), block), :]
            part = jnp.dot(left, dpre[:, h * hm : (h + 1) * hm], preferred_element_type=f32)
            gwp[h, to_dp] = part.reshape(ctxs, hd // count, hm)
            if d == 0:
                continue
            for c in list(range(1, ctxs)) + [0]:
                to_ctx = lax.rem(my_ctx + c, ctxs)
                copy = pltpu.make_async_remote_copy(
                    src_ref=gwp.at[h, to_dp, to_ctx],
                    dst_ref=recv1.at[h, d - 1, c],
                    send_sem=one_send.at[h, d - 1, c],
                    recv_sem=one_recv.at[h, d - 1, c],
                    device_id={"dp": to_dp},
                    device_id_type=MESH,
                )
                copy.start()
                sends.append(copy)
                stage_one[h, d, c] = copy

    def finish(h):
        ch = slice(h * hd, (h + 1) * hd)
        back = lax.dot_general(
            dpre[:, h * hm : (h + 1) * hm], w_ref[h], (((1,), (1,)), ((), ())),
            preferred_element_type=f32,
        )
        whole = (gxp[:, ch] + back).astype(bf16)
        gx_ref[:, ch] = jnp.dot(unperm, whole, preferred_element_type=f32).astype(bf16)
        out_ref[:, ch] = jnp.dot(unperm, outp[:, ch], preferred_element_type=f32).astype(bf16)

    for h in range(heads):
        finish(h)

    stage_two = {}
    for h in range(heads):
        for c in list(range(1, ctxs)) + [0]:
            to_ctx = lax.rem(my_ctx + c, ctxs)
            total = gwp[h, my_dp, to_ctx]
            for d in range(1, dps):
                stage_one[h, d, c].wait_recv()
                total = total + recv1[h, d - 1, c]
            if c == 0:
                gw_ref[h] = total
                continue
            sbuf[h, c - 1] = total
            copy = pltpu.make_async_remote_copy(
                src_ref=sbuf.at[h, c - 1],
                dst_ref=recv2.at[h, c - 1],
                send_sem=two_send.at[h, c - 1],
                recv_sem=two_recv.at[h, c - 1],
                device_id={"ctx": to_ctx},
                device_id_type=MESH,
            )
            copy.start()
            sends.append(copy)
            stage_two[h, c] = copy
    for h in range(heads):
        total = gw_ref[h]
        for c in range(1, ctxs):
            stage_two[h, c].wait_recv()
            total = total + recv2[h, c - 1]
        gw_ref[h] = total
    for copy in sends:
        copy.wait_send()


def per_device(dps, ctxs, inputs, doc_start, gate_weight, gate_bias, decay_rate, cotangent):
    batch_rows, rows, width = inputs.shape
    hd, heads, hm = gate_weight.shape
    count = dps * ctxs
    f32, bf16 = jnp.float32, jnp.bfloat16
    part = hd // count
    full = pltpu.VMEM((rows, width), f32)
    half = pltpu.VMEM((rows, width), bf16)
    vmem = pl.BlockSpec(memory_space=pltpu.VMEM)
    out, gx, gw = pl.pallas_call(
        functools.partial(kernel, dps, ctxs),
        out_shape=(
            jax.ShapeDtypeStruct((rows, width), bf16),
            jax.ShapeDtypeStruct((rows, width), bf16),
            jax.ShapeDtypeStruct((heads, part, hm), f32),
        ),
        in_specs=[vmem] * 6,
        out_specs=(vmem,) * 3,
        scratch_shapes=[
            full, half, pltpu.VMEM((width, rows), bf16), full, pltpu.VMEM((rows, hm), f32),
            full, full, full, full, full, full, full, full, full,
            half, pltpu.VMEM((rows, heads * hm), bf16), full,
            pltpu.VMEM((2, 2 * (width // 128), 128), f32),
            pltpu.VMEM((count - 1, 2 * (width // 128), 128), f32),
            pltpu.VMEM((heads, dps, ctxs, part, hm), f32),
            pltpu.VMEM((heads, dps - 1, ctxs, part, hm), f32),
            pltpu.VMEM((heads, ctxs - 1, part, hm), f32),
            pltpu.VMEM((heads, ctxs - 1, part, hm), f32),
            pltpu.SemaphoreType.DMA((count - 1,)),
            pltpu.SemaphoreType.DMA((count - 1,)),
            pltpu.SemaphoreType.DMA((heads, dps - 1, ctxs)),
            pltpu.SemaphoreType.DMA((heads, dps - 1, ctxs)),
            pltpu.SemaphoreType.DMA((heads, ctxs - 1)),
            pltpu.SemaphoreType.DMA((heads, ctxs - 1)),
        ],
        compiler_params=pltpu.CompilerParams(
            collective_id=0, has_side_effects=True, vmem_limit_bytes=32 * 1024 * 1024
        ),
    )(
        inputs.reshape(rows, width), doc_start.reshape(1, rows),
        jnp.transpose(gate_weight, (1, 0, 2)), gate_bias, decay_rate.reshape(1, width),
        cotangent.reshape(rows, width),
    )
    return (
        out.reshape(batch_rows, rows, width), gx.reshape(batch_rows, rows, width),
        jnp.transpose(gw, (1, 0, 2)),
    )


def solution(mesh):
    in_specs = (
        P(None, ("dp", "ctx"), "mp"),
        P(None, ("dp", "ctx")),
        P(None, "mp", None),
        P("mp", None),
        P("mp"),
        P(None, ("dp", "ctx"), "mp"),
    )
    out_specs = (
        P(None, ("dp", "ctx"), "mp"),
        P(None, ("dp", "ctx"), "mp"),
        P(("dp", "ctx"), "mp", None),
    )
    return jax.shard_map(
        functools.partial(per_device, mesh.shape["dp"], mesh.shape["ctx"]),
        mesh=mesh, in_specs=in_specs, out_specs=out_specs, check_vma=False,
    )
```

profile of v0, /device:TPU:0, one launch (start us, length us, event | category | flops | bytes accessed | tf_op | source)
XLA Modules:
  0.0 30.6 jit_solution(8236994401520320460)
XLA Ops:
  0.6 0.0 copy-start
  0.6 0.0 copy-start.1
  0.7 0.0 copy-start.2
  0.7 0.0 copy-start.3
  0.7 1.2 %copy.12 = bf16[256,2,512]{2,0,1:T(8,128)(2,1)S(1)} copy(bf16[256,2,512]{2,1,0:T(2,128)(2,1)} %param.8) | data formatting | bytes 1048576 | tf_op args[2]
  1.8 0.0 copy-start.4
  1.8 0.0 copy-done
  1.8 0.0 copy-done.1
  1.9 0.0 copy-done.2
  1.9 0.0 copy-done.3
  1.9 0.6 %copy-done.4 = s32[1,128]{1,0:T(1,128)S(1)} copy-done((s32[1,128]{1,0:T(1,128)S(1)}, s32[1,128]{1,0:T(1,128)}, u32[]{:S(2)}) %copy-start.4) | copy-done | bytes 536
  2.5 26.0 %shard_map.85 = (bf16[128,512]{1,0:T(8,128)(2,1)S(1)}, bf16[128,512]{1,0:T(8,128)(2,1)S(1)}, f32[2,32,512]{2,1,0:T(8,128)S(1)}) custom-call(bf16[128,512]{1,0:T(8,128)(2,1)S(1)} %bitcast.13, s32[1,128]{1,0:T(1,128)S(1)} %copy-done.4, bf16[2,256,512]{2,1,0:T(8,128)(2,1)S(1)} %bitcast.9, f32[2,512]{1,0:T(2,128)S(1)} %copy-done.2, f32[1,512]{1,0:T(1,128)S(1)} %bitcast.15, ...), custom_call_target="tpu_custom_call" | custom-call | tf_op jit(solution)/shard_map/pallas_call | solution.py:263
  28.5 0.8 %copy.10 = f32[32,2,512]{2,1,0:T(2,128)} copy(f32[32,2,512]{2,0,1:T(8,128)S(1)} %bitcast.12) | data formatting | bytes 262144
  29.2 0.7 %copy.15 = bf16[1,128,512]{2,1,0:T(8,128)(2,1)} copy(bf16[1,128,512]{2,1,0:T(8,128)(2,1)S(1)} %bitcast.11) | data formatting | bytes 262144
  29.9 0.7 %copy.16 = bf16[1,128,512]{2,1,0:T(8,128)(2,1)} copy(bf16[1,128,512]{2,1,0:T(8,128)(2,1)S(1)} %bitcast.10) | data formatting | bytes 262144
Async XLA Ops:
  0.6 1.2 %copy-start = (bf16[1,128,512]{2,1,0:T(8,128)(2,1)S(1)}, bf16[1,128,512]{2,1,0:T(8,128)(2,1)}, u32[]{:S(2)}) copy-start(bf16[1,128,512]{2,1,0:T(8,128)(2,1)} %param.6) | copy-start | bytes 393220
  0.6 1.2 %copy-start.1 = (bf16[1,128,512]{2,1,0:T(8,128)(2,1)S(1)}, bf16[1,128,512]{2,1,0:T(8,128)(2,1)}, u32[]{:S(2)}) copy-start(bf16[1,128,512]{2,1,0:T(8,128)(2,1)} %param.11) | copy-start | bytes 393220
  0.7 1.2 %copy-start.2 = (f32[2,512]{1,0:T(2,128)S(1)}, f32[2,512]{1,0:T(2,128)}, u32[]{:S(2)}) copy-start(f32[2,512]{1,0:T(2,128)} %bias_ref.1) | copy-start | bytes 12292
  0.7 1.2 %copy-start.3 = (f32[512]{0:T(512)S(1)}, f32[512]{0:T(512)}, u32[]{:S(2)}) copy-start(f32[512]{0:T(512)} %param.10) | copy-start | bytes 6148
  1.8 0.7 %copy-start.4 = (s32[1,128]{1,0:T(1,128)S(1)}, s32[1,128]{1,0:T(1,128)}, u32[]{:S(2)}) copy-start(s32[1,128]{1,0:T(1,128)} %doc_ref.1) | copy-start | bytes 1540
where the time goes:
time: 30.7 us; the launch traced here: 30.6 us
  Pallas kernels  26 us (85%)
  local copies, waits for them, and re-layouts  3.85 us (13%)
  between operations  0.72 us (2%)
    pallas_call x1, Pallas kernels, per_device(): pl.pallas_call(functools.partial(kernel, dps, ctxs), out_shape=(jax.Shape...  26 us
    unnamed x14, local copies, waits for them, and re-layouts  3.85 us

commit v1 on v0

--- a/solution.py
+++ b/solution.py
@@ -12,13 +12,24 @@
 
 
 def kernel(
-    dps, ctxs, x_ref, doc_ref, w_ref, bias_ref, rate_ref, g_ref, out_ref, gx_ref, gw_ref,
+    dps, ctxs, x_hbm, doc_hbm, w_hbm, bias_hbm, rate_hbm, g_hbm, out_hbm, gx_hbm, gw_hbm,
+    x_ref, doc_ref, w_pairs, bias_ref, rate_ref, g_ref, w_ref, loaded, gw_sum,
+    out_ref, gx_ref, gw_ref, stored,
     xf, xb, xt, gf, pre, carry_s, s_s, p_s, la_s, q_s, c1a_s, c1b_s, c2_s, c3_s, outp, dpre,
     gxp, sums, sums_in, gwp, recv1, sbuf, recv2,
     sum_send, sum_recv, one_send, one_recv, two_send, two_recv,
 ):
     rows, width = x_ref.shape
     heads, hd, hm = w_ref.shape
+    loads = [
+        pltpu.make_async_copy(source, target, loaded.at[k])
+        for k, (source, target) in enumerate((
+            (x_hbm, x_ref), (doc_hbm, doc_ref), (w_hbm, w_pairs), (bias_hbm, bias_ref),
+            (rate_hbm, rate_ref), (g_hbm, g_ref),
+        ))
+    ]
+    for load in loads:
+        load.start()
     count = dps * ctxs
     steps = rows // SUB
     my_dp, my_ctx = lax.axis_index("dp"), lax.axis_index("ctx")
@@ -39,11 +50,25 @@
     back_here = (col % SUB) * steps + col // SUB == row
     perm = jnp.where(here, 1.0, 0.0).astype(bf16)
     unperm = jnp.where(back_here, 1.0, 0.0).astype(bf16)
+    wide_row = lax.broadcasted_iota(jnp.int32, (hd, heads * hd), 0)
+    wide_col = lax.broadcasted_iota(jnp.int32, (hd, heads * hd), 1)
+    spread = [
+        jnp.where(wide_row * heads + h == wide_col, 1.0, 0.0).astype(bf16) for h in range(heads)
+    ]
+    loads[0].wait()
+    loads[1].wait()
     keep_col = 1.0 - jnp.sum(
         jnp.where(here, doc_ref[...].astype(f32), 0.0), axis=1, keepdims=True
     )
     xf[...] = jnp.dot(perm, x_ref[...], preferred_element_type=f32)
     xb[...] = xf[...].astype(bf16)
+    spread_x = [
+        jnp.dot(xb[:, h * hd : (h + 1) * hd], spread[h], preferred_element_type=f32).astype(bf16)
+        for h in range(heads)
+    ]
+    for load in loads[2:]:
+        load.wait()
+    w_all = w_pairs[...].reshape(hd * heads, hm)
     gf[...] = jnp.dot(perm, g_ref[...], preferred_element_type=f32)
     chunk = lax.broadcasted_iota(jnp.int32, (SUB, hd), 0)
 
@@ -51,7 +76,7 @@
     for h in range(heads):
         ch = slice(h * hd, (h + 1) * hd)
         pre[...] = (
-            jnp.dot(xb[:, ch], w_ref[h], preferred_element_type=f32) + bias_ref[h : h + 1, :]
+            jnp.dot(spread_x[h], w_all, preferred_element_type=f32) + bias_ref[h : h + 1, :]
         )
         rate8 = -8.0 * rate_ref[:, ch]
         state = prod = None
@@ -143,6 +168,7 @@
     for h in range(heads):
         ch = slice(h * hd, (h + 1) * hd)
         xt[ch, :] = jnp.transpose(xf[:, ch]).astype(bf16)
+        w_ref[h] = jnp.dot(spread[h], w_all, preferred_element_type=f32).astype(bf16)
 
     for copy in summaries:
         copy.wait_recv()
@@ -217,6 +243,14 @@
 
     for h in range(heads):
         finish(h)
+    stores = [
+        pltpu.make_async_copy(source, target, stored.at[k])
+        for k, (source, target) in enumerate(
+            ((out_ref, out_hbm), (gx_ref, gx_hbm), (gw_ref, gw_hbm))
+        )
+    ]
+    stores[0].start()
+    stores[1].start()
 
     stage_two = {}
     for h in range(heads):
@@ -227,7 +261,7 @@
                 stage_one[h, d, c].wait_recv()
                 total = total + recv1[h, d - 1, c]
             if c == 0:
-                gw_ref[h] = total
+                gw_sum[h] = total
                 continue
             sbuf[h, c - 1] = total
             copy = pltpu.make_async_remote_copy(
@@ -242,13 +276,29 @@
             sends.append(copy)
             stage_two[h, c] = copy
     for h in range(heads):
-        total = gw_ref[h]
+        total = gw_sum[h]
         for c in range(1, ctxs):
             stage_two[h, c].wait_recv()
             total = total + recv2[h, c - 1]
-        gw_ref[h] = total
+        gw_ref[:, h, :] = total
+    stores[2].start()
+    for store in stores:
+        store.wait()
     for copy in sends:
         copy.wait_send()
+
+
+def write_out(out_ref, gx_ref, gw_ref, out_hbm, gx_hbm, gw_hbm, done):
+    copies = [
+        pltpu.make_async_copy(source, target, done.at[k])
+        for k, (source, target) in enumerate(
+            ((out_ref, out_hbm), (gx_ref, gx_hbm), (gw_ref, gw_hbm))
+        )
+    ]
+    for copy in copies:
+        copy.start()
+    for copy in copies:
+        copy.wait()
 
 
 def per_device(dps, ctxs, inputs, doc_start, gate_weight, gate_bias, decay_rate, cotangent):
@@ -259,17 +309,23 @@
     part = hd // count
     full = pltpu.VMEM((rows, width), f32)
     half = pltpu.VMEM((rows, width), bf16)
-    vmem = pl.BlockSpec(memory_space=pltpu.VMEM)
-    out, gx, gw = pl.pallas_call(
+    hbm = pl.BlockSpec(memory_space=pltpu.HBM)
+    shapes = (
+        jax.ShapeDtypeStruct((rows, width), bf16),
+        jax.ShapeDtypeStruct((rows, width), bf16),
+        jax.ShapeDtypeStruct((part, heads, hm), f32),
+    )
+    held = pl.pallas_call(
         functools.partial(kernel, dps, ctxs),
-        out_shape=(
-            jax.ShapeDtypeStruct((rows, width), bf16),
-            jax.ShapeDtypeStruct((rows, width), bf16),
-            jax.ShapeDtypeStruct((heads, part, hm), f32),
-        ),
-        in_specs=[vmem] * 6,
-        out_specs=(vmem,) * 3,
+        out_shape=shapes,
+        in_specs=[hbm] * 6,
+        out_specs=(hbm,) * 3,
         scratch_shapes=[
+            half, pltpu.VMEM((1, rows), jnp.int32), pltpu.VMEM((hd, heads, hm), bf16),
+            pltpu.VMEM((heads, hm), f32), pltpu.VMEM((1, width), f32), half,
+            pltpu.VMEM((heads, hd, hm), bf16), pltpu.SemaphoreType.DMA((6,)),
+            pltpu.VMEM((heads, part, hm), f32), half, half, pltpu.VMEM((part, heads, hm), f32),
+            pltpu.SemaphoreType.DMA((3,)),
             full, half, pltpu.VMEM((width, rows), bf16), full, pltpu.VMEM((rows, hm), f32),
             full, full, full, full, full, full, full, full, full,
             half, pltpu.VMEM((rows, heads * hm), bf16), full,
@@ -287,17 +343,22 @@
             pltpu.SemaphoreType.DMA((heads, ctxs - 1)),
         ],
         compiler_params=pltpu.CompilerParams(
-            collective_id=0, has_side_effects=True, vmem_limit_bytes=32 * 1024 * 1024
+            collective_id=0, has_side_effects=True, vmem_limit_bytes=60 * 1024 * 1024
         ),
     )(
         inputs.reshape(rows, width), doc_start.reshape(1, rows),
-        jnp.transpose(gate_weight, (1, 0, 2)), gate_bias, decay_rate.reshape(1, width),
+        gate_weight, gate_bias, decay_rate.reshape(1, width),
         cotangent.reshape(rows, width),
     )
-    return (
-        out.reshape(batch_rows, rows, width), gx.reshape(batch_rows, rows, width),
-        jnp.transpose(gw, (1, 0, 2)),
-    )
+    out, gx, gw = pl.pallas_call(
+        write_out,
+        out_shape=shapes,
+        in_specs=[hbm] * 3,
+        out_specs=(hbm,) * 3,
+        scratch_shapes=[pltpu.SemaphoreType.DMA((3,))],
+        compiler_params=pltpu.CompilerParams(vmem_limit_bytes=60 * 1024 * 1024),
+    )(*held)
+    return (out.reshape(batch_rows, rows, width), gx.reshape(batch_rows, rows, width), gw)
 
 
 def solution(mesh):

time: 30.7 us -> 40.9 us (1.33)
  Pallas kernels: 26 us -> 40.1 us
  local copies, waits for them, and re-layouts: 3.85 us -> 0 us
    pallas_call x1 -> x2, Pallas kernels: 26 us -> 40.1 us  [the longest x1 27 us: per_device(): pl.pallas_call(functools.partial(kernel, dps, ctxs), out_shape=shapes, in...]
    unnamed x14 -> x0, local copies, waits for them, and re-layouts: 3.85 us -> none
where the time goes in v1:
time: 40.9 us; the launch traced here: 40.7 us
  Pallas kernels  40.1 us (98%)
  between operations  0.64 us (2%)
    pallas_call x1, Pallas kernels, per_device(): pl.pallas_call(functools.partial(kernel, dps, ctxs), out_shape=shapes, in...  27 us
    pallas_call x1, Pallas kernels, per_device(): pl.pallas_call(write_out, out_shape=shapes, in_specs=[hbm] * 3, out_specs...  13 us

profile of v1, /device:TPU:0, one launch (start us, length us, event | category | flops | bytes accessed | tf_op | source)
XLA Modules:
  0.0 40.7 jit_solution(11694283761175973422)
XLA Ops:
  0.6 27.0 %shard_map.85 = (bf16[128,512]{1,0:T(8,128)(2,1)}, bf16[128,512]{1,0:T(8,128)(2,1)}, f32[32,2,512]{2,1,0:T(2,128)}) custom-call(bf16[128,512]{1,0:T(8,128)(2,1)} %bitcast.5, s32[1,128]{1,0:T(1,128)} %doc_hbm.1, bf16[256,2,512]{2,1,0:T(2,128)(2,1)} %w_hbm.1, f32[2,512]{1,0:T(2,128)} %bias_hbm.1, f32[1,512]{1,0:T(1,128)} %bitcast.7, bf16[128,512]{1,0:T(8,128)(2,1)} %bitcast.6), custom_call_target="tpu_custom_call" | custom-call | tf_op jit(solution)/shard_map/pallas_call | solution.py:318
  27.7 13.0 %shard_map.86 = (bf16[128,512]{1,0:T(8,128)(2,1)}, bf16[128,512]{1,0:T(8,128)(2,1)}, f32[32,2,512]{2,1,0:T(2,128)}) custom-call(bf16[128,512]{1,0:T(8,128)(2,1)} %get-tuple-element.9.out_ref, bf16[128,512]{1,0:T(8,128)(2,1)} %get-tuple-element.10.gx_ref, f32[32,2,512]{2,1,0:T(2,128)} %get-tuple-element.11.gw_ref), custom_call_target="tpu_custom_call" | custom-call | tf_op jit(solution)/shard_map/pallas_call | solution.py:353

commit v2 on v1

v2 whole, which is shorter than its diff:
```python
import functools

import jax
import jax.numpy as jnp
from jax import lax
from jax.experimental import pallas as pl
from jax.experimental.pallas import tpu as pltpu
from jax.sharding import PartitionSpec as P

MESH = pl.DeviceIdType.MESH
SUB = 8


def orders(bits):
    return [()] if bits == 0 else [(f,) + o for f in (1, 0) for o in orders(bits - 1)]


def number(flips):
    return sum(f << i for i, f in enumerate(flips))


def kernel(
    dps, ctxs, early, x_hbm, doc_hbm, w_hbm, bias_hbm, rate_hbm, g_hbm, out_hbm, gx_hbm, gw_hbm,
    x_ref, doc_ref, w_pairs, bias_ref, rate_ref, g_ref, w_ref, loaded, gw_sum,
    out_ref, gx_ref, gw_ref, stored,
    x_out, g_out, doc_out, x_in, g_in, doc_in,
    xf, xb, xt, gf, pre, carry_s, s_s, p_s, la_s, q_s, c1a_s, c1b_s, c2_s, c3_s, outp, dpre,
    gxp, sums, gwp, recv1, sbuf, recv2,
    early_send, early_recv, sum_send, sum_recv, one_send, one_recv, two_send, two_recv,
):
    rows, width = x_ref.shape
    heads, hd, hm = w_ref.shape
    loads = [
        pltpu.make_async_copy(source, target, loaded.at[k])
        for k, (source, target) in enumerate((
            (x_hbm, x_ref), (doc_hbm, doc_ref), (g_hbm, g_ref), (w_hbm, w_pairs),
            (bias_hbm, bias_ref), (rate_hbm, rate_ref),
        ))
    ]
    for load in loads:
        load.start()
    count = dps * ctxs
    steps = rows // SUB
    bits = ctxs.bit_length() - 1
    my_dp, my_ctx = lax.axis_index("dp"), lax.axis_index("ctx")
    me = my_dp * ctxs + my_ctx
    f32, bf16 = jnp.float32, jnp.bfloat16
    sends = []

    barrier = pltpu.get_barrier_semaphore()
    for d in range(1, count):
        to = lax.rem(me + d, count)
        pl.semaphore_signal(
            barrier, inc=1, device_id={"dp": to // ctxs, "ctx": lax.rem(to, ctxs)},
            device_id_type=MESH,
        )

    def send(source, target, send_sem, recv_sem, device):
        copy = pltpu.make_async_remote_copy(
            src_ref=source, dst_ref=target, send_sem=send_sem, recv_sem=recv_sem,
            device_id=device, device_id_type=MESH,
        )
        copy.start()
        sends.append(copy)
        return copy

    row = lax.broadcasted_iota(jnp.int32, (rows, rows), 0)
    col = lax.broadcasted_iota(jnp.int32, (rows, rows), 1)
    here = (row % SUB) * steps + row // SUB == col
    back_here = (col % SUB) * steps + col // SUB == row
    perm = jnp.where(here, 1.0, 0.0).astype(bf16)
    unperm = jnp.where(back_here, 1.0, 0.0).astype(bf16)
    wide_row = lax.broadcasted_iota(jnp.int32, (hd, heads * hd), 0)
    wide_col = lax.broadcasted_iota(jnp.int32, (hd, heads * hd), 1)
    spread = [
        jnp.where(wide_row * heads + h == wide_col, 1.0, 0.0).astype(bf16) for h in range(heads)
    ]
    chunk = lax.broadcasted_iota(jnp.int32, (SUB, hd), 0)

    for load in loads[:3]:
        load.wait()
    doc_float = doc_ref[...].astype(f32)
    if early:
        x_out[...] = x_ref[:, : early * hd].astype(f32)
        g_out[...] = g_ref[:, : early * hd].astype(f32)
        doc_out[...] = jnp.broadcast_to(doc_float, doc_out.shape)
    pl.semaphore_wait(barrier, count - 1)
    early_copies = []
    if early:
        other = {"dp": 1 - my_dp}
        for k, (source, target) in enumerate(((doc_out, doc_in), (x_out, x_in), (g_out, g_in))):
            early_copies.append(
                send(source, target, early_send.at[k], early_recv.at[k], other)
            )

    def keep_of(doc):
        return 1.0 - jnp.sum(jnp.where(here, doc, 0.0), axis=1, keepdims=True)

    def gates(u, h, keep_col, w_all):
        ch = slice(u * hd, (u + 1) * hd)
        spread_x = jnp.dot(xb[:, ch], spread[h], preferred_element_type=f32).astype(bf16)
        pre[...] = (
            jnp.dot(spread_x, w_all, preferred_element_type=f32) + bias_ref[h : h + 1, :]
        )
        rate8 = -8.0 * rate_ref[:, h * hd : (h + 1) * hd]
        state = prod = None
        for i in range(steps):
            rs = slice(i * SUB, (i + 1) * SUB)
            x = xf[rs, ch]
            keep = jnp.broadcast_to(keep_col[rs], (SUB, hd))
            kept = keep > 0.5
            rgate = 0.5 * jnp.tanh(0.5 * pre[rs, :hd]) + 0.5
            igate = 0.5 * jnp.tanh(0.5 * pre[rs, hd:]) + 0.5
            decay = jnp.exp(rate8 * rgate)
            square = decay * decay
            inside = 1.0 - square + 0.01
            inverse = lax.rsqrt(inside)
            carry = decay * keep
            scale = jnp.where(kept, inside * inverse, 1.0)
            gated = igate * x
            drive = scale * gated
            c1 = rate8 * rgate * (1.0 - rgate)
            carry_s[rs, ch] = carry
            c1a_s[rs, ch] = carry * c1
            c1b_s[rs, ch] = gated * jnp.where(kept, -square * inverse, 0.0) * c1
            c2_s[rs, ch] = drive * (1.0 - igate)
            if u < heads:
                c3_s[rs, ch] = scale * igate
            if i == 0:
                state, prod = drive, carry
            else:
                state, prod = carry * state + drive, carry * prod
            s_s[rs, ch] = state
            p_s[rs, ch] = prod
        return state, prod

    def chunks(u, state, prod):
        ch = slice(u * hd, (u + 1) * hd)
        adj = gf[(steps - 1) * SUB :, ch]
        tail = jnp.ones((SUB, hd), f32)
        la_s[(steps - 1) * SUB :, ch] = adj
        q_s[(steps - 1) * SUB :, ch] = tail
        for i in range(steps - 2, -1, -1):
            rs = slice(i * SUB, (i + 1) * SUB)
            after = carry_s[(i + 1) * SUB : (i + 2) * SUB, ch]
            adj = gf[rs, ch] + after * adj
            tail = after * tail
            la_s[rs, ch] = adj
            q_s[rs, ch] = tail
        fs, fp = state, prod
        bu, bp = carry_s[:SUB, ch] * adj, prod
        s = 1
        while s < SUB:
            ok = chunk >= s
            rolled_p, rolled_s = pltpu.roll(fp, s, 0), pltpu.roll(fs, s, 0)
            fs = jnp.where(ok, fp * rolled_s + fs, fs)
            fp = jnp.where(ok, fp * rolled_p, fp)
            ok = chunk < SUB - s
            rolled_p, rolled_s = pltpu.roll(bp, SUB - s, 0), pltpu.roll(bu, SUB - s, 0)
            bu = jnp.where(ok, bp * rolled_s + bu, bu)
            bp = jnp.where(ok, bp * rolled_p, bp)
            s *= 2
        ends = (
            jnp.where(chunk >= 1, pltpu.roll(fp, 1, 0), 1.0),
            jnp.where(chunk >= 1, pltpu.roll(fs, 1, 0), 0.0),
            jnp.where(chunk < SUB - 1, pltpu.roll(bp, SUB - 1, 0), 1.0),
            jnp.where(chunk < SUB - 1, pltpu.roll(bu, SUB - 1, 0), 0.0),
        )
        return ends, (fp[SUB - 1 :], fs[SUB - 1 :], bu[:1])

    per = hd // 128
    half = width // 128
    keep_col = keep_of(doc_float)
    xf[:, :width] = jnp.dot(perm, x_ref[...], preferred_element_type=f32)
    xb[:, :width] = xf[:, :width].astype(bf16)
    gf[:, :width] = jnp.dot(perm, g_ref[...], preferred_element_type=f32)
    for load in loads[3:]:
        load.wait()
    w_all = w_pairs[...].reshape(hd * heads, hm)
    ends = {}
    for h in range(heads):
        ends[h], whole = chunks(h, *gates(h, h, keep_col, w_all))
        for k, value in enumerate(whole):
            for l in range(per):
                at = k * half + h * per + l
                sums[me, at : at + 1] = value[:, l * 128 : (l + 1) * 128]

    summaries = []
    for d in range(1, count):
        to = lax.rem(me + d, count)
        summaries.append(send(
            sums.at[me], sums.at[me], sum_send.at[d - 1], sum_recv.at[d - 1],
            {"dp": to // ctxs, "ctx": lax.rem(to, ctxs)},
        ))

    for h in range(heads):
        xt[h * hd : (h + 1) * hd, :] = jnp.transpose(xf[:, h * hd : (h + 1) * hd]).astype(bf16)
        w_ref[h] = jnp.dot(spread[h], w_all, preferred_element_type=f32).astype(bf16)
    if early:
        extra = slice(width, width + early * hd)
        early_copies[0].wait_recv()
        early_copies[1].wait_recv()
        keep_other = keep_of(doc_in[:1])
        xf[:, extra] = jnp.dot(perm, x_in[...].astype(bf16), preferred_element_type=f32)
        xb[:, extra] = xf[:, extra].astype(bf16)
        xt[extra, :] = jnp.transpose(xf[:, extra]).astype(bf16)
        firsts = [gates(heads + e, e, keep_other, w_all) for e in range(early)]
        early_copies[2].wait_recv()
        gf[:, extra] = jnp.dot(perm, g_in[...].astype(bf16), preferred_element_type=f32)
        for e in range(early):
            ends[heads + e], _ = chunks(heads + e, *firsts[e])

    for copy in summaries:
        copy.wait_recv()

    def entering(place):
        state_in = jnp.zeros((half, 128), f32)
        adj_in = jnp.zeros((half, 128), f32)
        for s in range(count):
            longer = sums[s, :half] * state_in + sums[s, half : 2 * half]
            state_in = jnp.where(s < place, longer, state_in)
            t = count - 1 - s
            longer = sums[t, :half] * adj_in + sums[t, 2 * half :]
            adj_in = jnp.where(t > place, longer, adj_in)
        return state_in, adj_in

    def lanes_of(value, h):
        return jnp.concatenate([value[h * per + l : h * per + l + 1] for l in range(per)], axis=1)

    def second(u, h, enter):
        ch = slice(u * hd, (u + 1) * hd)
        ex_p, ex_s, ex_q, ex_u = ends[u]
        start = ex_s + ex_p * lanes_of(enter[0], h)
        prev = start
        later = ex_u + ex_q * lanes_of(enter[1], h)
        for i in range(0, steps, 2):
            got = []
            for j in (i, i + 1):
                rs = slice(j * SUB, (j + 1) * SUB)
                state = s_s[rs, ch] + p_s[rs, ch] * start
                adj = la_s[rs, ch] + q_s[rs, ch] * later
                dgate = adj * (c1a_s[rs, ch] * prev + c1b_s[rs, ch])
                own = (state, adj * c3_s[rs, ch]) if u < heads else ()
                got.append((dgate, adj * c2_s[rs, ch]) + own)
                prev = state
            both = slice(i * SUB, (i + 2) * SUB)
            pair = [jnp.concatenate(two) for two in zip(*got)]
            dpre[both, u * hm : u * hm + hd] = pair[0].astype(bf16)
            dpre[both, u * hm + hd : (u + 1) * hm] = pair[1].astype(bf16)
            if u < heads:
                outp[both, ch] = pair[2].astype(bf16)
                gxp[both, ch] = pair[3]

    block = ctxs * (hd // count)

    def product(u, to_dp):
        left = xt[pl.ds(pl.multiple_of(u * hd + to_dp * block, block), block), :]
        return jnp.dot(left, dpre[:, u * hm : (u + 1) * hm], preferred_element_type=f32)

    def shard(flips):
        place = 0
        for i, f in enumerate(flips):
            bit = (my_ctx // (1 << i)) % 2
            place = place + (1 << i) * (1 - bit if f else bit)
        return place

    order = orders(bits)
    stage_one = {}
    stage_two = {}

    def first_stage(h):
        for d in range(1, dps):
            to_dp = lax.rem(my_dp + d, dps)
            gwp[h, to_dp] = product(h, to_dp).reshape(ctxs, hd // count, hm)
            for flips in order:
                k = number(flips)
                stage_one[h, d, k] = send(
                    gwp.at[h, to_dp, shard(flips)], recv1.at[h, d - 1, k],
                    one_send.at[h, d - 1, k], one_recv.at[h, d - 1, k], {"dp": to_dp},
                )

    def mine(h):
        part = product(h, my_dp)
        if h < early:
            part = part + product(heads + h, my_dp)
        gwp[h, my_dp] = part.reshape(ctxs, hd // count, hm)

    def slot(step, flips):
        return sum(1 << (bits - 1 - i) for i in range(step)) + number(flips[step + 1 :])

    def second_stage(h, flips):
        step = flips.index(1) if 1 in flips else bits
        total = gwp[h, my_dp, shard(flips)]
        if h >= early:
            for d in range(1, dps):
                stage_one[h, d, number(flips)].wait_recv()
                total = total + recv1[h, d - 1, number(flips)]
        for i in range(step):
            stage_two[h, slot(i, flips)].wait_recv()
            total = total + recv2[h, slot(i, flips)]
        if step == bits:
            gw_ref[:, h, :] = total
            return
        k = slot(step, flips)
        sbuf[h, k] = total
        bit = (my_ctx // (1 << step)) % 2
        stage_two[h, k] = send(
            sbuf.at[h, k], recv2.at[h, k], two_send.at[h, k], two_recv.at[h, k],
            {"ctx": my_ctx + (1 << step) * (1 - 2 * bit)},
        )

    def finish(h):
        ch = slice(h * hd, (h + 1) * hd)
        back = lax.dot_general(
            dpre[:, h * hm : (h + 1) * hm], w_ref[h], (((1,), (1,)), ((), ())),
            preferred_element_type=f32,
        )
        whole = (gxp[:, ch] + back).astype(bf16)
        gx_ref[:, ch] = jnp.dot(unperm, whole, preferred_element_type=f32).astype(bf16)
        out_ref[:, ch] = jnp.dot(unperm, outp[:, ch], preferred_element_type=f32).astype(bf16)

    enter = entering(me)
    for h in range(early, heads):
        second(h, h, enter)
        first_stage(h)
    enter_other = entering((1 - my_dp) * ctxs + my_ctx) if early else None
    for h in range(early):
        second(h, h, enter)
        second(heads + h, h, enter_other)
        mine(h)
        for flips in order[: ctxs // 2]:
            second_stage(h, flips)
    for h in range(early, heads):
        mine(h)
    for h in range(heads):
        finish(h)
    stores = [
        pltpu.make_async_copy(source, target, stored.at[k])
        for k, (source, target) in enumerate(
            ((out_ref, out_hbm), (gx_ref, gx_hbm), (gw_ref, gw_hbm))
        )
    ]
    stores[0].start()
    stores[1].start()
    for h in range(early):
        for flips in order[ctxs // 2 : -1]:
            second_stage(h, flips)
    for h in range(early, heads):
        for flips in order[:-1]:
            second_stage(h, flips)
    for h in range(heads):
        second_stage(h, order[-1])
    stores[2].start()
    for store in stores:
        store.wait()
    for copy in sends:
        copy.wait_send()


def write_out(out_in, gx_in, gw_in, out_hbm, gx_hbm, gw_hbm, out_ref, gx_ref, gw_ref, came, done):
    ins = [
        pltpu.make_async_copy(source, target, came.at[k])
        for k, (source, target) in enumerate(((out_in, out_ref), (gx_in, gx_ref), (gw_in, gw_ref)))
    ]
    outs = [
        pltpu.make_async_copy(source, target, done.at[k])
        for k, (source, target) in enumerate(
            ((out_ref, out_hbm), (gx_ref, gx_hbm), (gw_ref, gw_hbm))
        )
    ]
    for copy in ins:
        copy.start()
    for copy, after in zip(ins, outs):
        copy.wait()
        after.start()
    for copy in outs:
        copy.wait()


def per_device(dps, ctxs, inputs, doc_start, gate_weight, gate_bias, decay_rate, cotangent):
    batch_rows, rows, width = inputs.shape
    hd, heads, hm = gate_weight.shape
    count = dps * ctxs
    early = 1 if dps == 2 and heads > 1 else 0
    lent = max(early, 1) * hd
    f32, bf16 = jnp.float32, jnp.bfloat16
    part = hd // count
    full = pltpu.VMEM((rows, width + lent), f32)
    half = pltpu.VMEM((rows, width), bf16)
    sent = pltpu.VMEM((rows, lent), f32)
    lane_rows = 3 * (width // 128)
    hbm = pl.BlockSpec(memory_space=pltpu.HBM)
    params = dict(vmem_limit_bytes=60 * 1024 * 1024)
    shapes = (
        jax.ShapeDtypeStruct((rows, width), bf16),
        jax.ShapeDtypeStruct((rows, width), bf16),
        jax.ShapeDtypeStruct((part, heads, hm), f32),
    )
    held = pl.pallas_call(
        functools.partial(kernel, dps, ctxs, early),
        out_shape=shapes,
        in_specs=[hbm] * 6,
        out_specs=(hbm,) * 3,
        scratch_shapes=[
            half, pltpu.VMEM((1, rows), jnp.int32), pltpu.VMEM((hd, heads, hm), bf16),
            pltpu.VMEM((heads, hm), f32), pltpu.VMEM((1, width), f32), half,
            pltpu.VMEM((heads, hd, hm), bf16), pltpu.SemaphoreType.DMA((6,)),
            pltpu.VMEM((heads, part, hm), f32), half, half, pltpu.VMEM((part, heads, hm), f32),
            pltpu.SemaphoreType.DMA((3,)),
            sent, sent, pltpu.VMEM((SUB, rows), f32), sent, sent, pltpu.VMEM((SUB, rows), f32),
            full, pltpu.VMEM((rows, width + lent), bf16), pltpu.VMEM((width + lent, rows), bf16),
            full, pltpu.VMEM((rows, hm), f32),
            full, full, full, full, full, full, full, full, full,
            half, pltpu.VMEM((rows, (heads + max(early, 1)) * hm), bf16),
            pltpu.VMEM((rows, width), f32),
            pltpu.VMEM((count, lane_rows, 128), f32),
            pltpu.VMEM((heads, dps, ctxs, part, hm), f32),
            pltpu.VMEM((heads, dps - 1, ctxs, part, hm), f32),
            pltpu.VMEM((heads, ctxs - 1, part, hm), f32),
            pltpu.VMEM((heads, ctxs - 1, part, hm), f32),
            pltpu.SemaphoreType.DMA((3,)),
            pltpu.SemaphoreType.DMA((3,)),
            pltpu.SemaphoreType.DMA((count - 1,)),
            pltpu.SemaphoreType.DMA((count - 1,)),
            pltpu.SemaphoreType.DMA((heads, dps - 1, ctxs)),
            pltpu.SemaphoreType.DMA((heads, dps - 1, ctxs)),
            pltpu.SemaphoreType.DMA((heads, ctxs - 1)),
            pltpu.SemaphoreType.DMA((heads, ctxs - 1)),
        ],
        compiler_params=pltpu.CompilerParams(collective_id=0, has_side_effects=True, **params),
    )(
        inputs.reshape(rows, width), doc_start.reshape(1, rows), gate_weight, gate_bias,
        decay_rate.reshape(1, width), cotangent.reshape(rows, width),
    )
    out, gx, gw = pl.pallas_call(
        write_out,
        out_shape=shapes,
        in_specs=[hbm] * 3,
        out_specs=(hbm,) * 3,
        scratch_shapes=[
            half, half, pltpu.VMEM((part, heads, hm), f32),
            pltpu.SemaphoreType.DMA((3,)), pltpu.SemaphoreType.DMA((3,)),
        ],
        compiler_params=pltpu.CompilerParams(**params),
    )(*held)
    return (out.reshape(batch_rows, rows, width), gx.reshape(batch_rows, rows, width), gw)


def solution(mesh):
    in_specs = (
        P(None, ("dp", "ctx"), "mp"),
        P(None, ("dp", "ctx")),
        P(None, "mp", None),
        P("mp", None),
        P("mp"),
        P(None, ("dp", "ctx"), "mp"),
    )
    out_specs = (
        P(None, ("dp", "ctx"), "mp"),
        P(None, ("dp", "ctx"), "mp"),
        P(("dp", "ctx"), "mp", None),
    )
    return jax.shard_map(
        functools.partial(per_device, mesh.shape["dp"], mesh.shape["ctx"]),
        mesh=mesh, in_specs=in_specs, out_specs=out_specs, check_vma=False,
    )
```

time: 40.9 us -> 29.1 us (0.71)
  Pallas kernels: 40.1 us -> 28.3 us
    pallas_call x1, Pallas kernels: 13 us -> 1.74 us  [per_device(): pl.pallas_call(write_out, out_shape=shapes, in_specs=[hbm] * 3, out_specs...]
    pallas_call x1, Pallas kernels: 27 us -> 26.5 us  [per_device(): pl.pallas_call(functools.partial(kernel, dps, ctxs, early), out_shape=sha...]
where the time goes in v2:
time: 29.1 us; the launch traced here: 28.9 us
  Pallas kernels  28.3 us (97%)
  between operations  0.64 us (2%)
    pallas_call x1, Pallas kernels, per_device(): pl.pallas_call(functools.partial(kernel, dps, ctxs, early), out_shape=sha...  26.5 us
    pallas_call x1, Pallas kernels, per_device(): pl.pallas_call(write_out, out_shape=shapes, in_specs=[hbm] * 3, out_specs...  1.74 us

profile of v2, /device:TPU:0, one launch (start us, length us, event | category | flops | bytes accessed | tf_op | source)
XLA Modules:
  0.0 28.9 jit_solution(9329133879165411884)
XLA Ops:
  0.6 26.5 %shard_map.85 = (bf16[128,512]{1,0:T(8,128)(2,1)}, bf16[128,512]{1,0:T(8,128)(2,1)}, f32[32,2,512]{2,1,0:T(2,128)}) custom-call(bf16[128,512]{1,0:T(8,128)(2,1)} %bitcast.5, s32[1,128]{1,0:T(1,128)} %doc_hbm.1, bf16[256,2,512]{2,1,0:T(2,128)(2,1)} %w_hbm.1, f32[2,512]{1,0:T(2,128)} %bias_hbm.1, f32[1,512]{1,0:T(1,128)} %bitcast.7, bf16[128,512]{1,0:T(8,128)(2,1)} %bitcast.6), custom_call_target="tpu_custom_call" | custom-call | tf_op jit(solution)/shard_map/pallas_call | solution.py:399
  27.2 1.7 %shard_map.86 = (bf16[128,512]{1,0:T(8,128)(2,1)}, bf16[128,512]{1,0:T(8,128)(2,1)}, f32[32,2,512]{2,1,0:T(2,128)}) custom-call(bf16[128,512]{1,0:T(8,128)(2,1)} %get-tuple-element.9.out_in, bf16[128,512]{1,0:T(8,128)(2,1)} %get-tuple-element.10.gx_in, f32[32,2,512]{2,1,0:T(2,128)} %get-tuple-element.11.gw_in), custom_call_target="tpu_custom_call" | custom-call | tf_op jit(solution)/shard_map/pallas_call | solution.py:435

commit v3 on v2

--- a/solution.py
+++ b/solution.py
@@ -66,8 +66,9 @@
 
     row = lax.broadcasted_iota(jnp.int32, (rows, rows), 0)
     col = lax.broadcasted_iota(jnp.int32, (rows, rows), 1)
-    here = (row % SUB) * steps + row // SUB == col
-    back_here = (col % SUB) * steps + col // SUB == row
+    low = SUB.bit_length() - 1
+    here = (row & (SUB - 1)) * steps + (row >> low) == col
+    back_here = (col & (SUB - 1)) * steps + (col >> low) == row
     perm = jnp.where(here, 1.0, 0.0).astype(bf16)
     unperm = jnp.where(back_here, 1.0, 0.0).astype(bf16)
     wide_row = lax.broadcasted_iota(jnp.int32, (hd, heads * hd), 0)
@@ -96,12 +97,15 @@
     def keep_of(doc):
         return 1.0 - jnp.sum(jnp.where(here, doc, 0.0), axis=1, keepdims=True)
 
-    def gates(u, h, keep_col, w_all):
+    def project(u, h, w_all):
         ch = slice(u * hd, (u + 1) * hd)
         spread_x = jnp.dot(xb[:, ch], spread[h], preferred_element_type=f32).astype(bf16)
-        pre[...] = (
+        pre[:, u * hm : (u + 1) * hm] = (
             jnp.dot(spread_x, w_all, preferred_element_type=f32) + bias_ref[h : h + 1, :]
         )
+
+    def gates(u, h, keep_col):
+        ch = slice(u * hd, (u + 1) * hd)
         rate8 = -8.0 * rate_ref[:, h * hd : (h + 1) * hd]
         state = prod = None
         for i in range(steps):
@@ -109,8 +113,8 @@
             x = xf[rs, ch]
             keep = jnp.broadcast_to(keep_col[rs], (SUB, hd))
             kept = keep > 0.5
-            rgate = 0.5 * jnp.tanh(0.5 * pre[rs, :hd]) + 0.5
-            igate = 0.5 * jnp.tanh(0.5 * pre[rs, hd:]) + 0.5
+            rgate = 0.5 * jnp.tanh(0.5 * pre[rs, u * hm : u * hm + hd]) + 0.5
+            igate = 0.5 * jnp.tanh(0.5 * pre[rs, u * hm + hd : (u + 1) * hm]) + 0.5
             decay = jnp.exp(rate8 * rgate)
             square = decay * decay
             inside = 1.0 - square + 0.01
@@ -179,7 +183,9 @@
     w_all = w_pairs[...].reshape(hd * heads, hm)
     ends = {}
     for h in range(heads):
-        ends[h], whole = chunks(h, *gates(h, h, keep_col, w_all))
+        project(h, h, w_all)
+    for h in range(heads):
+        ends[h], whole = chunks(h, *gates(h, h, keep_col))
         for k, value in enumerate(whole):
             for l in range(per):
                 at = k * half + h * per + l
@@ -195,20 +201,6 @@
 
     for h in range(heads):
         xt[h * hd : (h + 1) * hd, :] = jnp.transpose(xf[:, h * hd : (h + 1) * hd]).astype(bf16)
-        w_ref[h] = jnp.dot(spread[h], w_all, preferred_element_type=f32).astype(bf16)
-    if early:
-        extra = slice(width, width + early * hd)
-        early_copies[0].wait_recv()
-        early_copies[1].wait_recv()
-        keep_other = keep_of(doc_in[:1])
-        xf[:, extra] = jnp.dot(perm, x_in[...].astype(bf16), preferred_element_type=f32)
-        xb[:, extra] = xf[:, extra].astype(bf16)
-        xt[extra, :] = jnp.transpose(xf[:, extra]).astype(bf16)
-        firsts = [gates(heads + e, e, keep_other, w_all) for e in range(early)]
-        early_copies[2].wait_recv()
-        gf[:, extra] = jnp.dot(perm, g_in[...].astype(bf16), preferred_element_type=f32)
-        for e in range(early):
-            ends[heads + e], _ = chunks(heads + e, *firsts[e])
 
     for copy in summaries:
         copy.wait_recv()
@@ -323,16 +315,32 @@
     for h in range(early, heads):
         second(h, h, enter)
         first_stage(h)
-    enter_other = entering((1 - my_dp) * ctxs + my_ctx) if early else None
     for h in range(early):
         second(h, h, enter)
-        second(heads + h, h, enter_other)
-        mine(h)
-        for flips in order[: ctxs // 2]:
-            second_stage(h, flips)
+    if early:
+        extra = slice(width, width + early * hd)
+        early_copies[0].wait_recv()
+        early_copies[1].wait_recv()
+        keep_other = keep_of(doc_in[:1])
+        xf[:, extra] = jnp.dot(perm, x_in[...].astype(bf16), preferred_element_type=f32)
+        xb[:, extra] = xf[:, extra].astype(bf16)
+        xt[extra, :] = jnp.transpose(xf[:, extra]).astype(bf16)
+        for e in range(early):
+            project(heads + e, e, w_all)
+        firsts = [gates(heads + e, e, keep_other) for e in range(early)]
+        enter_other = entering((1 - my_dp) * ctxs + my_ctx)
+        early_copies[2].wait_recv()
+        gf[:, extra] = jnp.dot(perm, g_in[...].astype(bf16), preferred_element_type=f32)
+        for e in range(early):
+            ends[heads + e], _ = chunks(heads + e, *firsts[e])
+            second(heads + e, e, enter_other)
+            mine(e)
+            for flips in order[: ctxs // 2]:
+                second_stage(e, flips)
     for h in range(early, heads):
         mine(h)
     for h in range(heads):
+        w_ref[h] = jnp.dot(spread[h], w_all, preferred_element_type=f32).astype(bf16)
         finish(h)
     stores = [
         pltpu.make_async_copy(source, target, stored.at[k])
@@ -409,7 +417,7 @@
             pltpu.SemaphoreType.DMA((3,)),
             sent, sent, pltpu.VMEM((SUB, rows), f32), sent, sent, pltpu.VMEM((SUB, rows), f32),
             full, pltpu.VMEM((rows, width + lent), bf16), pltpu.VMEM((width + lent, rows), bf16),
-            full, pltpu.VMEM((rows, hm), f32),
+            full, pltpu.VMEM((rows, (heads + max(early, 1)) * hm), f32),
             full, full, full, full, full, full, full, full, full,
             half, pltpu.VMEM((rows, (heads + max(early, 1)) * hm), bf16),
             pltpu.VMEM((rows, width), f32),

time: 29.1 us -> 29.5 us (1.014)
  Pallas kernels: 28.3 us -> 28.7 us
    pallas_call x1, Pallas kernels: 26.5 us -> 27 us  [per_device(): pl.pallas_call(functools.partial(kernel, dps, ctxs, early), out_shape=sha...]
where the time goes in v3:
time: 29.5 us; the launch traced here: 29.4 us
  Pallas kernels  28.7 us (97%)
  between operations  0.64 us (2%)
    pallas_call x1, Pallas kernels, per_device(): pl.pallas_call(functools.partial(kernel, dps, ctxs, early), out_shape=sha...  27 us
    pallas_call x1, Pallas kernels, per_device(): pl.pallas_call(write_out, out_shape=shapes, in_specs=[hbm] * 3, out_specs...  1.74 us

profile of v3, /device:TPU:0, one launch (start us, length us, event | category | flops | bytes accessed | tf_op | source)
XLA Modules:
  0.0 29.4 jit_solution(15714412670051043936)
XLA Ops:
  0.6 27.0 %shard_map.85 = (bf16[128,512]{1,0:T(8,128)(2,1)}, bf16[128,512]{1,0:T(8,128)(2,1)}, f32[32,2,512]{2,1,0:T(2,128)}) custom-call(bf16[128,512]{1,0:T(8,128)(2,1)} %bitcast.5, s32[1,128]{1,0:T(1,128)} %doc_hbm.1, bf16[256,2,512]{2,1,0:T(2,128)(2,1)} %w_hbm.1, f32[2,512]{1,0:T(2,128)} %bias_hbm.1, f32[1,512]{1,0:T(1,128)} %bitcast.7, bf16[128,512]{1,0:T(8,128)(2,1)} %bitcast.6), custom_call_target="tpu_custom_call" | custom-call | tf_op jit(solution)/shard_map/pallas_call | solution.py:407
  27.6 1.7 %shard_map.86 = (bf16[128,512]{1,0:T(8,128)(2,1)}, bf16[128,512]{1,0:T(8,128)(2,1)}, f32[32,2,512]{2,1,0:T(2,128)}) custom-call(bf16[128,512]{1,0:T(8,128)(2,1)} %get-tuple-element.9.out_in, bf16[128,512]{1,0:T(8,128)(2,1)} %get-tuple-element.10.gx_in, f32[32,2,512]{2,1,0:T(2,128)} %get-tuple-element.11.gw_in), custom_call_target="tpu_custom_call" | custom-call | tf_op jit(solution)/shard_map/pallas_call | solution.py:443

commit v4 on v2

--- a/solution.py
+++ b/solution.py
@@ -66,8 +66,9 @@
 
     row = lax.broadcasted_iota(jnp.int32, (rows, rows), 0)
     col = lax.broadcasted_iota(jnp.int32, (rows, rows), 1)
-    here = (row % SUB) * steps + row // SUB == col
-    back_here = (col % SUB) * steps + col // SUB == row
+    low = SUB.bit_length() - 1
+    here = (row & (SUB - 1)) * steps + (row >> low) == col
+    back_here = (col & (SUB - 1)) * steps + (col >> low) == row
     perm = jnp.where(here, 1.0, 0.0).astype(bf16)
     unperm = jnp.where(back_here, 1.0, 0.0).astype(bf16)
     wide_row = lax.broadcasted_iota(jnp.int32, (hd, heads * hd), 0)
@@ -96,12 +97,15 @@
     def keep_of(doc):
         return 1.0 - jnp.sum(jnp.where(here, doc, 0.0), axis=1, keepdims=True)
 
-    def gates(u, h, keep_col, w_all):
+    def project(u, h, w_all):
         ch = slice(u * hd, (u + 1) * hd)
         spread_x = jnp.dot(xb[:, ch], spread[h], preferred_element_type=f32).astype(bf16)
-        pre[...] = (
+        pre[:, u * hm : (u + 1) * hm] = (
             jnp.dot(spread_x, w_all, preferred_element_type=f32) + bias_ref[h : h + 1, :]
         )
+
+    def gates(u, h, keep_col):
+        ch = slice(u * hd, (u + 1) * hd)
         rate8 = -8.0 * rate_ref[:, h * hd : (h + 1) * hd]
         state = prod = None
         for i in range(steps):
@@ -109,8 +113,8 @@
             x = xf[rs, ch]
             keep = jnp.broadcast_to(keep_col[rs], (SUB, hd))
             kept = keep > 0.5
-            rgate = 0.5 * jnp.tanh(0.5 * pre[rs, :hd]) + 0.5
-            igate = 0.5 * jnp.tanh(0.5 * pre[rs, hd:]) + 0.5
+            rgate = 0.5 * jnp.tanh(0.5 * pre[rs, u * hm : u * hm + hd]) + 0.5
+            igate = 0.5 * jnp.tanh(0.5 * pre[rs, u * hm + hd : (u + 1) * hm]) + 0.5
             decay = jnp.exp(rate8 * rgate)
             square = decay * decay
             inside = 1.0 - square + 0.01
@@ -179,7 +183,9 @@
     w_all = w_pairs[...].reshape(hd * heads, hm)
     ends = {}
     for h in range(heads):
-        ends[h], whole = chunks(h, *gates(h, h, keep_col, w_all))
+        project(h, h, w_all)
+    for h in range(heads):
+        ends[h], whole = chunks(h, *gates(h, h, keep_col))
         for k, value in enumerate(whole):
             for l in range(per):
                 at = k * half + h * per + l
@@ -195,6 +201,8 @@
 
     for h in range(heads):
         xt[h * hd : (h + 1) * hd, :] = jnp.transpose(xf[:, h * hd : (h + 1) * hd]).astype(bf16)
+
+    for h in range(heads):
         w_ref[h] = jnp.dot(spread[h], w_all, preferred_element_type=f32).astype(bf16)
     if early:
         extra = slice(width, width + early * hd)
@@ -204,7 +212,9 @@
         xf[:, extra] = jnp.dot(perm, x_in[...].astype(bf16), preferred_element_type=f32)
         xb[:, extra] = xf[:, extra].astype(bf16)
         xt[extra, :] = jnp.transpose(xf[:, extra]).astype(bf16)
-        firsts = [gates(heads + e, e, keep_other, w_all) for e in range(early)]
+        for e in range(early):
+            project(heads + e, e, w_all)
+        firsts = [gates(heads + e, e, keep_other) for e in range(early)]
         early_copies[2].wait_recv()
         gf[:, extra] = jnp.dot(perm, g_in[...].astype(bf16), preferred_element_type=f32)
         for e in range(early):
@@ -323,30 +333,35 @@
     for h in range(early, heads):
         second(h, h, enter)
         first_stage(h)
-    enter_other = entering((1 - my_dp) * ctxs + my_ctx) if early else None
     for h in range(early):
         second(h, h, enter)
-        second(heads + h, h, enter_other)
-        mine(h)
-        for flips in order[: ctxs // 2]:
-            second_stage(h, flips)
-    for h in range(early, heads):
-        mine(h)
-    for h in range(heads):
-        finish(h)
     stores = [
         pltpu.make_async_copy(source, target, stored.at[k])
         for k, (source, target) in enumerate(
             ((out_ref, out_hbm), (gx_ref, gx_hbm), (gw_ref, gw_hbm))
         )
     ]
-    stores[0].start()
-    stores[1].start()
+    enter_other = entering((1 - my_dp) * ctxs + my_ctx) if early else None
+    for e in range(early):
+        second(heads + e, e, enter_other)
+        mine(e)
+        for flips in order[: ctxs // 2]:
+            second_stage(e, flips)
+    for h in range(early, heads):
+        mine(h)
+    finish(0)
+    for h in range(early, heads):
+        for flips in order[: ctxs // 2]:
+            second_stage(h, flips)
     for h in range(early):
         for flips in order[ctxs // 2 : -1]:
             second_stage(h, flips)
+    for h in range(1, heads):
+        finish(h)
+    stores[0].start()
+    stores[1].start()
     for h in range(early, heads):
-        for flips in order[:-1]:
+        for flips in order[ctxs // 2 : -1]:
             second_stage(h, flips)
     for h in range(heads):
         second_stage(h, order[-1])
@@ -409,7 +424,7 @@
             pltpu.SemaphoreType.DMA((3,)),
             sent, sent, pltpu.VMEM((SUB, rows), f32), sent, sent, pltpu.VMEM((SUB, rows), f32),
             full, pltpu.VMEM((rows, width + lent), bf16), pltpu.VMEM((width + lent, rows), bf16),
-            full, pltpu.VMEM((rows, hm), f32),
+            full, pltpu.VMEM((rows, (heads + max(early, 1)) * hm), f32),
             full, full, full, full, full, full, full, full, full,
             half, pltpu.VMEM((rows, (heads + max(early, 1)) * hm), bf16),
             pltpu.VMEM((rows, width), f32),

time: 29.1 us -> 28.6 us (0.983)
  Pallas kernels: 28.3 us -> 27.8 us
    pallas_call x1, Pallas kernels: 26.5 us -> 26.1 us  [per_device(): pl.pallas_call(functools.partial(kernel, dps, ctxs, early), out_shape=sha...]
where the time goes in v4:
time: 28.6 us; the launch traced here: 28.5 us
  Pallas kernels  27.8 us (97%)
  between operations  0.64 us (2%)
    pallas_call x1, Pallas kernels, per_device(): pl.pallas_call(functools.partial(kernel, dps, ctxs, early), out_shape=sha...  26.1 us
    pallas_call x1, Pallas kernels, per_device(): pl.pallas_call(write_out, out_shape=shapes, in_specs=[hbm] * 3, out_specs...  1.74 us

profile of v4, /device:TPU:0, one launch (start us, length us, event | category | flops | bytes accessed | tf_op | source)
XLA Modules:
  0.0 28.5 jit_solution(4959786392531371401)
XLA Ops:
  0.6 26.1 %shard_map.85 = (bf16[128,512]{1,0:T(8,128)(2,1)}, bf16[128,512]{1,0:T(8,128)(2,1)}, f32[32,2,512]{2,1,0:T(2,128)}) custom-call(bf16[128,512]{1,0:T(8,128)(2,1)} %bitcast.5, s32[1,128]{1,0:T(1,128)} %doc_hbm.1, bf16[256,2,512]{2,1,0:T(2,128)(2,1)} %w_hbm.1, f32[2,512]{1,0:T(2,128)} %bias_hbm.1, f32[1,512]{1,0:T(1,128)} %bitcast.7, bf16[128,512]{1,0:T(8,128)(2,1)} %bitcast.6), custom_call_target="tpu_custom_call" | custom-call | tf_op jit(solution)/shard_map/pallas_call | solution.py:414
  26.7 1.7 %shard_map.86 = (bf16[128,512]{1,0:T(8,128)(2,1)}, bf16[128,512]{1,0:T(8,128)(2,1)}, f32[32,2,512]{2,1,0:T(2,128)}) custom-call(bf16[128,512]{1,0:T(8,128)(2,1)} %get-tuple-element.9.out_in, bf16[128,512]{1,0:T(8,128)(2,1)} %get-tuple-element.10.gx_in, f32[32,2,512]{2,1,0:T(2,128)} %get-tuple-element.11.gw_in), custom_call_target="tpu_custom_call" | custom-call | tf_op jit(solution)/shard_map/pallas_call | solution.py:450

commit v5 on v4

--- a/solution.py
+++ b/solution.py
@@ -23,7 +23,7 @@
     dps, ctxs, early, x_hbm, doc_hbm, w_hbm, bias_hbm, rate_hbm, g_hbm, out_hbm, gx_hbm, gw_hbm,
     x_ref, doc_ref, w_pairs, bias_ref, rate_ref, g_ref, w_ref, loaded, gw_sum,
     out_ref, gx_ref, gw_ref, stored,
-    x_out, g_out, doc_out, x_in, g_in, doc_in,
+    x_out, g_out, doc_out, x_in, g_in, doc_in, ends_in,
     xf, xb, xt, gf, pre, carry_s, s_s, p_s, la_s, q_s, c1a_s, c1b_s, c2_s, c3_s, outp, dpre,
     gxp, sums, gwp, recv1, sbuf, recv2,
     early_send, early_recv, sum_send, sum_recv, one_send, one_recv, two_send, two_recv,
@@ -42,6 +42,8 @@
     count = dps * ctxs
     steps = rows // SUB
     bits = ctxs.bit_length() - 1
+    lend = lax.rem(lax.axis_index("mp"), 2) == 0
+    keeps = jnp.logical_not(lend)
     my_dp, my_ctx = lax.axis_index("dp"), lax.axis_index("ctx")
     me = my_dp * ctxs + my_ctx
     f32, bf16 = jnp.float32, jnp.bfloat16
@@ -55,11 +57,14 @@
             device_id_type=MESH,
         )
 
-    def send(source, target, send_sem, recv_sem, device):
-        copy = pltpu.make_async_remote_copy(
+    def describe(source, target, send_sem, recv_sem, device):
+        return pltpu.make_async_remote_copy(
             src_ref=source, dst_ref=target, send_sem=send_sem, recv_sem=recv_sem,
             device_id=device, device_id_type=MESH,
         )
+
+    def send(*what):
+        copy = describe(*what)
         copy.start()
         sends.append(copy)
         return copy
@@ -86,13 +91,17 @@
         g_out[...] = g_ref[:, : early * hd].astype(f32)
         doc_out[...] = jnp.broadcast_to(doc_float, doc_out.shape)
     pl.semaphore_wait(barrier, count - 1)
-    early_copies = []
-    if early:
-        other = {"dp": 1 - my_dp}
-        for k, (source, target) in enumerate(((doc_out, doc_in), (x_out, x_in), (g_out, g_in))):
-            early_copies.append(
-                send(source, target, early_send.at[k], early_recv.at[k], other)
-            )
+    early_copies = [
+        describe(source, target, early_send.at[k], early_recv.at[k], {"dp": 1 - my_dp})
+        for k, (source, target) in enumerate(((doc_out, doc_in), (x_out, x_in), (g_out, g_in)))
+    ] if early else []
+    if early:
+
+        @pl.when(lend)
+        def _():
+            for copy in early_copies:
+                copy.start()
+
 
     def keep_of(doc):
         return 1.0 - jnp.sum(jnp.where(here, doc, 0.0), axis=1, keepdims=True)
@@ -205,20 +214,25 @@
     for h in range(heads):
         w_ref[h] = jnp.dot(spread[h], w_all, preferred_element_type=f32).astype(bf16)
     if early:
-        extra = slice(width, width + early * hd)
-        early_copies[0].wait_recv()
-        early_copies[1].wait_recv()
-        keep_other = keep_of(doc_in[:1])
-        xf[:, extra] = jnp.dot(perm, x_in[...].astype(bf16), preferred_element_type=f32)
-        xb[:, extra] = xf[:, extra].astype(bf16)
-        xt[extra, :] = jnp.transpose(xf[:, extra]).astype(bf16)
-        for e in range(early):
-            project(heads + e, e, w_all)
-        firsts = [gates(heads + e, e, keep_other) for e in range(early)]
-        early_copies[2].wait_recv()
-        gf[:, extra] = jnp.dot(perm, g_in[...].astype(bf16), preferred_element_type=f32)
-        for e in range(early):
-            ends[heads + e], _ = chunks(heads + e, *firsts[e])
+
+        @pl.when(lend)
+        def _():
+            extra = slice(width, width + early * hd)
+            early_copies[0].wait_recv()
+            early_copies[1].wait_recv()
+            keep_other = keep_of(doc_in[:1])
+            xf[:, extra] = jnp.dot(perm, x_in[...].astype(bf16), preferred_element_type=f32)
+            xb[:, extra] = xf[:, extra].astype(bf16)
+            xt[extra, :] = jnp.transpose(xf[:, extra]).astype(bf16)
+            for e in range(early):
+                project(heads + e, e, w_all)
+            firsts = [gates(heads + e, e, keep_other) for e in range(early)]
+            early_copies[2].wait_recv()
+            gf[:, extra] = jnp.dot(perm, g_in[...].astype(bf16), preferred_element_type=f32)
+            for e in range(early):
+                found, _ = chunks(heads + e, *firsts[e])
+                for k, value in enumerate(found):
+                    ends_in[e, k] = value
 
     for copy in summaries:
         copy.wait_recv()
@@ -239,7 +253,7 @@
 
     def second(u, h, enter):
         ch = slice(u * hd, (u + 1) * hd)
-        ex_p, ex_s, ex_q, ex_u = ends[u]
+        ex_p, ex_s, ex_q, ex_u = ends[u] if u < heads else [ends_in[u - heads, k] for k in range(4)]
         start = ex_s + ex_p * lanes_of(enter[0], h)
         prev = start
         later = ex_u + ex_q * lanes_of(enter[1], h)
@@ -278,33 +292,54 @@
     stage_one = {}
     stage_two = {}
 
+    shards = {flips: shard(flips) for flips in order}
+    partners = [lax.rem(my_dp + d, dps) for d in range(dps)]
+    for h in range(heads):
+        for d in range(1, dps):
+            for flips in order:
+                k = number(flips)
+                stage_one[h, d, k] = describe(
+                    gwp.at[h, partners[d], shards[flips]], recv1.at[h, d - 1, k],
+                    one_send.at[h, d - 1, k], one_recv.at[h, d - 1, k], {"dp": partners[d]},
+                )
+
     def first_stage(h):
         for d in range(1, dps):
-            to_dp = lax.rem(my_dp + d, dps)
-            gwp[h, to_dp] = product(h, to_dp).reshape(ctxs, hd // count, hm)
+            gwp[h, partners[d]] = product(h, partners[d]).reshape(ctxs, hd // count, hm)
             for flips in order:
-                k = number(flips)
-                stage_one[h, d, k] = send(
-                    gwp.at[h, to_dp, shard(flips)], recv1.at[h, d - 1, k],
-                    one_send.at[h, d - 1, k], one_recv.at[h, d - 1, k], {"dp": to_dp},
-                )
-
-    def mine(h):
+                stage_one[h, d, number(flips)].start()
+
+    def mine(h, both=False):
         part = product(h, my_dp)
-        if h < early:
+        if both:
             part = part + product(heads + h, my_dp)
         gwp[h, my_dp] = part.reshape(ctxs, hd // count, hm)
 
     def slot(step, flips):
         return sum(1 << (bits - 1 - i) for i in range(step)) + number(flips[step + 1 :])
 
-    def second_stage(h, flips):
+    for h in range(heads):
+        for flips in order[:-1]:
+            step = flips.index(1)
+            bit = (my_ctx // (1 << step)) % 2
+            k = slot(step, flips)
+            stage_two[h, k] = describe(
+                sbuf.at[h, k], recv2.at[h, k], two_send.at[h, k], two_recv.at[h, k],
+                {"ctx": my_ctx + (1 << step) * (1 - 2 * bit)},
+            )
+
+    def arrived(h, flips):
+        for d in range(1, dps):
+            stage_one[h, d, number(flips)].wait_recv()
+            gwp[h, my_dp, shards[flips]] += recv1[h, d - 1, number(flips)]
+
+    def second_stage(h, flips, lent=None):
         step = flips.index(1) if 1 in flips else bits
-        total = gwp[h, my_dp, shard(flips)]
-        if h >= early:
-            for d in range(1, dps):
-                stage_one[h, d, number(flips)].wait_recv()
-                total = total + recv1[h, d - 1, number(flips)]
+        if h >= early or lent is False:
+            arrived(h, flips)
+        elif lent is None:
+            pl.when(keeps)(functools.partial(arrived, h, flips))
+        total = gwp[h, my_dp, shards[flips]]
         for i in range(step):
             stage_two[h, slot(i, flips)].wait_recv()
             total = total + recv2[h, slot(i, flips)]
@@ -313,11 +348,7 @@
             return
         k = slot(step, flips)
         sbuf[h, k] = total
-        bit = (my_ctx // (1 << step)) % 2
-        stage_two[h, k] = send(
-            sbuf.at[h, k], recv2.at[h, k], two_send.at[h, k], two_recv.at[h, k],
-            {"ctx": my_ctx + (1 << step) * (1 - 2 * bit)},
-        )
+        stage_two[h, k].start()
 
     def finish(h):
         ch = slice(h * hd, (h + 1) * hd)
@@ -342,34 +373,84 @@
         )
     ]
     enter_other = entering((1 - my_dp) * ctxs + my_ctx) if early else None
-    for e in range(early):
-        second(heads + e, e, enter_other)
-        mine(e)
-        for flips in order[: ctxs // 2]:
-            second_stage(e, flips)
+    near, far = order[: ctxs // 2], order[ctxs // 2 : -1]
+    if early:
+
+        @pl.when(lend)
+        def _():
+            for e in range(early):
+                second(heads + e, e, enter_other)
+                mine(e, True)
+                for flips in near:
+                    second_stage(e, flips, True)
+
+        @pl.when(keeps)
+        def _():
+            for e in range(early):
+                first_stage(e)
+                mine(e)
+
     for h in range(early, heads):
         mine(h)
     finish(0)
     for h in range(early, heads):
-        for flips in order[: ctxs // 2]:
+        for flips in near:
             second_stage(h, flips)
-    for h in range(early):
-        for flips in order[ctxs // 2 : -1]:
-            second_stage(h, flips)
+    if early:
+
+        @pl.when(lend)
+        def _():
+            for e in range(early):
+                for flips in far:
+                    second_stage(e, flips, True)
+
     for h in range(1, heads):
         finish(h)
     stores[0].start()
     stores[1].start()
+    if early:
+
+        @pl.when(keeps)
+        def _():
+            for e in range(early):
+                for flips in near:
+                    second_stage(e, flips, False)
+
     for h in range(early, heads):
-        for flips in order[ctxs // 2 : -1]:
+        for flips in far:
             second_stage(h, flips)
-    for h in range(heads):
+    if early:
+
+        @pl.when(keeps)
+        def _():
+            for e in range(early):
+                for flips in far:
+                    second_stage(e, flips, False)
+
+    for h in range(early, heads):
+        second_stage(h, order[-1])
+    for h in range(early):
         second_stage(h, order[-1])
     stores[2].start()
     for store in stores:
         store.wait()
-    for copy in sends:
+    for copy in sends + list(stage_two.values()):
         copy.wait_send()
+    for (h, _, _), copy in stage_one.items():
+        if h >= early:
+            copy.wait_send()
+    if early:
+
+        @pl.when(lend)
+        def _():
+            for copy in early_copies:
+                copy.wait_send()
+
+        @pl.when(keeps)
+        def _():
+            for (h, _, _), copy in stage_one.items():
+                if h < early:
+                    copy.wait_send()
 
 
 def write_out(out_in, gx_in, gw_in, out_hbm, gx_hbm, gw_hbm, out_ref, gx_ref, gw_ref, came, done):
@@ -423,6 +504,7 @@
             pltpu.VMEM((heads, part, hm), f32), half, half, pltpu.VMEM((part, heads, hm), f32),
             pltpu.SemaphoreType.DMA((3,)),
             sent, sent, pltpu.VMEM((SUB, rows), f32), sent, sent, pltpu.VMEM((SUB, rows), f32),
+            pltpu.VMEM((max(early, 1), 4, SUB, hd), f32),
             full, pltpu.VMEM((rows, width + lent), bf16), pltpu.VMEM((width + lent, rows), bf16),
             full, pltpu.VMEM((rows, (heads + max(early, 1)) * hm), f32),
             full, full, full, full, full, full, full, full, full,

time: 28.6 us -> 29.2 us (1.021)
  the two profiles are of different devices: /device:TPU:0 before, /device:TPU:1 now
where the time goes in v5:
time: 29.2 us; the launch traced here: 29.1 us
  Pallas kernels  28.4 us (97%)
  between operations  0.64 us (2%)
    pallas_call x1, Pallas kernels, per_device(): pl.pallas_call(functools.partial(kernel, dps, ctxs, early), out_shape=sha...  26.7 us
    pallas_call x1, Pallas kernels, per_device(): pl.pallas_call(write_out, out_shape=shapes, in_specs=[hbm] * 3, out_specs...  1.74 us

profile of v5, /device:TPU:1, one launch (start us, length us, event | category | flops | bytes accessed | tf_op | source)
XLA Modules:
  0.0 29.1 jit_solution(13034387510147613722)
XLA Ops:
  0.6 26.7 %shard_map.85 = (bf16[128,512]{1,0:T(8,128)(2,1)}, bf16[128,512]{1,0:T(8,128)(2,1)}, f32[32,2,512]{2,1,0:T(2,128)}) custom-call(bf16[128,512]{1,0:T(8,128)(2,1)} %bitcast.5, s32[1,128]{1,0:T(1,128)} %doc_hbm.1, bf16[256,2,512]{2,1,0:T(2,128)(2,1)} %w_hbm.1, f32[2,512]{1,0:T(2,128)} %bias_hbm.1, f32[1,512]{1,0:T(1,128)} %bitcast.7, bf16[128,512]{1,0:T(8,128)(2,1)} %bitcast.6), custom_call_target="tpu_custom_call" | custom-call | tf_op jit(solution)/shard_map/pallas_call | solution.py:495
  27.3 1.7 %shard_map.86 = (bf16[128,512]{1,0:T(8,128)(2,1)}, bf16[128,512]{1,0:T(8,128)(2,1)}, f32[32,2,512]{2,1,0:T(2,128)}) custom-call(bf16[128,512]{1,0:T(8,128)(2,1)} %get-tuple-element.9.out_in, bf16[128,512]{1,0:T(8,128)(2,1)} %get-tuple-element.10.gx_in, f32[32,2,512]{2,1,0:T(2,128)} %get-tuple-element.11.gw_in), custom_call_target="tpu_custom_call" | custom-call | tf_op jit(solution)/shard_map/pallas_call | solution.py:532

commit v6 on v4

--- a/solution.py
+++ b/solution.py
@@ -89,10 +89,17 @@
     early_copies = []
     if early:
         other = {"dp": 1 - my_dp}
-        for k, (source, target) in enumerate(((doc_out, doc_in), (x_out, x_in), (g_out, g_in))):
+        for k, (source, target) in enumerate(((doc_out, doc_in), (x_out, x_in))):
             early_copies.append(
                 send(source, target, early_send.at[k], early_recv.at[k], other)
             )
+        first = lax.rem(lax.axis_index("mp"), 2) == 0
+        early_copies.append(pltpu.make_async_remote_copy(
+            src_ref=g_out, dst_ref=g_in, send_sem=early_send.at[2], recv_sem=early_recv.at[2],
+            device_id=other, device_id_type=MESH,
+        ))
+        sends.append(early_copies[2])
+        pl.when(first)(early_copies[2].start)
 
     def keep_of(doc):
         return 1.0 - jnp.sum(jnp.where(here, doc, 0.0), axis=1, keepdims=True)
@@ -198,6 +205,9 @@
             sums.at[me], sums.at[me], sum_send.at[d - 1], sum_recv.at[d - 1],
             {"dp": to // ctxs, "ctx": lax.rem(to, ctxs)},
         ))
+
+    if early:
+        pl.when(jnp.logical_not(first))(early_copies[2].start)
 
     for h in range(heads):
         xt[h * hd : (h + 1) * hd, :] = jnp.transpose(xf[:, h * hd : (h + 1) * hd]).astype(bf16)

time: 28.6 us -> 28.6 us (level)
  no operation moved by 1% of the time
where the time goes in v6:
time: 28.6 us; the launch traced here: 28.5 us
  Pallas kernels  27.8 us (97%)
  between operations  0.64 us (2%)
    pallas_call x1, Pallas kernels, per_device(): pl.pallas_call(functools.partial(kernel, dps, ctxs, early), out_shape=sha...  26.1 us
    pallas_call x1, Pallas kernels, per_device(): pl.pallas_call(write_out, out_shape=shapes, in_specs=[hbm] * 3, out_specs...  1.74 us

profile of v6, /device:TPU:0, one launch (start us, length us, event | category | flops | bytes accessed | tf_op | source)
XLA Modules:
  0.0 28.5 jit_solution(16795349325202946470)
XLA Ops:
  0.6 26.1 %shard_map.85 = (bf16[128,512]{1,0:T(8,128)(2,1)}, bf16[128,512]{1,0:T(8,128)(2,1)}, f32[32,2,512]{2,1,0:T(2,128)}) custom-call(bf16[128,512]{1,0:T(8,128)(2,1)} %bitcast.5, s32[1,128]{1,0:T(1,128)} %doc_hbm.1, bf16[256,2,512]{2,1,0:T(2,128)(2,1)} %w_hbm.1, f32[2,512]{1,0:T(2,128)} %bias_hbm.1, f32[1,512]{1,0:T(1,128)} %bitcast.7, bf16[128,512]{1,0:T(8,128)(2,1)} %bitcast.6), custom_call_target="tpu_custom_call" | custom-call | tf_op jit(solution)/shard_map/pallas_call | solution.py:424
  26.7 1.7 %shard_map.86 = (bf16[128,512]{1,0:T(8,128)(2,1)}, bf16[128,512]{1,0:T(8,128)(2,1)}, f32[32,2,512]{2,1,0:T(2,128)}) custom-call(bf16[128,512]{1,0:T(8,128)(2,1)} %get-tuple-element.9.out_in, bf16[128,512]{1,0:T(8,128)(2,1)} %get-tuple-element.10.gx_in, f32[32,2,512]{2,1,0:T(2,128)} %get-tuple-element.11.gw_in), custom_call_target="tpu_custom_call" | custom-call | tf_op jit(solution)/shard_map/pallas_call | solution.py:460

commit v7 on v4

--- a/solution.py
+++ b/solution.py
@@ -396,7 +396,7 @@
     batch_rows, rows, width = inputs.shape
     hd, heads, hm = gate_weight.shape
     count = dps * ctxs
-    early = 1 if dps == 2 and heads > 1 else 0
+    early = 0
     lent = max(early, 1) * hd
     f32, bf16 = jnp.float32, jnp.bfloat16
     part = hd // count

time: 28.6 us -> 32.7 us (1.14)
  Pallas kernels: 27.8 us -> 31.9 us
    pallas_call x1, Pallas kernels: 26.1 us -> 30.2 us  [per_device(): pl.pallas_call(functools.partial(kernel, dps, ctxs, early), out_shape=sha...]
where the time goes in v7:
time: 32.7 us; the launch traced here: 32.5 us
  Pallas kernels  31.9 us (98%)
  between operations  0.64 us (2%)
    pallas_call x1, Pallas kernels, per_device(): pl.pallas_call(functools.partial(kernel, dps, ctxs, early), out_shape=sha...  30.2 us
    pallas_call x1, Pallas kernels, per_device(): pl.pallas_call(write_out, out_shape=shapes, in_specs=[hbm] * 3, out_specs...  1.74 us

profile of v7, /device:TPU:0, one launch (start us, length us, event | category | flops | bytes accessed | tf_op | source)
XLA Modules:
  0.0 32.5 jit_solution(9693145200658497153)
XLA Ops:
  0.6 30.2 %shard_map.85 = (bf16[128,512]{1,0:T(8,128)(2,1)}, bf16[128,512]{1,0:T(8,128)(2,1)}, f32[32,2,512]{2,1,0:T(2,128)}) custom-call(bf16[128,512]{1,0:T(8,128)(2,1)} %bitcast.5, s32[1,128]{1,0:T(1,128)} %doc_hbm.1, bf16[256,2,512]{2,1,0:T(2,128)(2,1)} %w_hbm.1, f32[2,512]{1,0:T(2,128)} %bias_hbm.1, f32[1,512]{1,0:T(1,128)} %bitcast.7, bf16[128,512]{1,0:T(8,128)(2,1)} %bitcast.6), custom_call_target="tpu_custom_call" | custom-call | tf_op jit(solution)/shard_map/pallas_call | solution.py:414
  30.8 1.7 %shard_map.86 = (bf16[128,512]{1,0:T(8,128)(2,1)}, bf16[128,512]{1,0:T(8,128)(2,1)}, f32[32,2,512]{2,1,0:T(2,128)}) custom-call(bf16[128,512]{1,0:T(8,128)(2,1)} %get-tuple-element.9.out_in, bf16[128,512]{1,0:T(8,128)(2,1)} %get-tuple-element.10.gx_in, f32[32,2,512]{2,1,0:T(2,128)} %get-tuple-element.11.gw_in), custom_call_target="tpu_custom_call" | custom-call | tf_op jit(solution)/shard_map/pallas_call | solution.py:450
